TPU v7x, 256 devices: a whole 4x4x8 slice. The times are simulated.
256 devices in a mesh: segment: 32 (over z, x), col: 8 (over y, core).
Axes of the slice: x: 4, y: 4, z: 8, core: 2. Of those that a mesh axis runs over, the one named last changes fastest.
Arguments:
- acts: float32 [128, 65536], P(None, 'col'), may hold values from 0 to 8
- tiles: bfloat16 [32, 768, 128, 128], P('segment', 'col'), may hold values from -0.625 to 0.625
- tile_row: int32 [32, 768], P('segment', 'col'), may hold values from 0 to 511, as said below
- tile_col: int32 [32, 768], P('segment', 'col'), may hold values from 0 to 63
- tile_count: int32 [32, 8], P('segment', 'col'), may hold values from 72 to 96, as said below
- bias: float32 [32, 65536], P('segment', 'col'), may hold values from -1 to 1
Outputs:
- final_acts: float32 [128, 65536], P('segment', 'col')
Inputs may be any that keep to these rules, and one draw needn't show every extreme that they name: `tile_row`: a slot of column shard c reads an input block from c * 64 - 32 to (c + 1) * 64 + 31, within the layer; in every layer each shard has valid slots at both ends of that band. `tile_count`: in every layer some column shard has all 96 slots valid; the valid slots of a shard are its first ones.
All inputs are finite; a program needn't handle non-finite values.
Results may differ from a plain program's by a relative error of at most 0.0006.
Values sent between devices are 32-bit elements; how exact they have to be, the bound alone decides.
A program may use at most 64 MiB of HBM per device.

v0:
```python
import jax
import jax.numpy as jnp
from jax import lax
from jax.sharding import PartitionSpec as P

REACH = 32
MICRO = 16


def extended_2(cells, sides, width):
    for axis, dim in sides:
        count = lax.axis_size(axis)
        ends = count - 1
        head = lax.slice_in_dim(cells, 0, width, axis=dim)
        tail = lax.slice_in_dim(cells, cells.shape[dim] - width, cells.shape[dim], axis=dim)
        cells = jnp.concatenate(
            [
                lax.ppermute(tail, axis, [(i, (i + 1) % count) for i in range(ends)]),
                cells,
                lax.ppermute(head, axis, [((i + 1) % count, i) for i in range(ends)]),
            ],
            axis=dim,
        )
    return cells


def shifted(block, axis, distance):
    devices = range(lax.axis_size(axis))
    route = [(i - distance, i) for i in devices if i - distance in devices]
    return lax.ppermute(block, axis, route)


def local(acts, tiles, tile_row, tile_col, tile_count, bias):
    segments = lax.axis_size("segment")
    segment = lax.axis_index("segment")
    column = lax.axis_index("col")
    weights = tiles[0].astype(jnp.float32)
    capacity = weights.shape[0]
    tile_size = weights.shape[-1]
    width = acts.shape[1]
    own_blocks = width // tile_size
    rim = REACH * tile_size
    micro_rows = acts.shape[0] // MICRO
    valid = jnp.arange(capacity, dtype=jnp.int32) < tile_count[0, 0]
    local_rows = tile_row[0] - column * own_blocks + REACH
    selector = (
        (tile_col[0][:, None] == jnp.arange(own_blocks, dtype=jnp.int32)[None, :]) & valid[:, None]
    ).astype(jnp.float32)
    shift_row = bias[0]

    def layer(extended):
        blocks = extended.reshape(micro_rows, own_blocks + 2 * REACH, tile_size)
        picked = jnp.take(blocks, local_rows, axis=1)
        partial_sum = jnp.einsum("rsk,skj->rsj", picked, weights, precision=lax.Precision.HIGHEST)
        total = jnp.einsum("rsj,sc->rcj", partial_sum, selector, precision=lax.Precision.HIGHEST)
        total = total.reshape(micro_rows, width) + shift_row[None, :]
        return jnp.clip(total, 0.0, 32.0)

    input_ext = extended_2(acts, (("col", 1),), rim)
    steps = MICRO + segments - 1

    def first_input(index):
        return lax.dynamic_slice_in_dim(input_ext, index * micro_rows, micro_rows, 0)

    def record(results, output, index, live):
        start = index * micro_rows
        former = lax.dynamic_slice_in_dim(results, start, micro_rows, 0)
        keep = live & (segment == segments - 1)
        return lax.dynamic_update_slice_in_dim(results, jnp.where(keep, output, former), start, 0)

    results = jnp.zeros(acts.shape, jnp.float32)

    def advance(step, carry):
        received, stored = carry
        micro = step - segment
        live = (micro >= 0) & (micro < MICRO)
        index = jnp.clip(micro, 0, MICRO - 1)
        rimmed = extended_2(received, (("col", 1),), rim)
        current = jnp.where(segment == 0, first_input(index), rimmed)
        output = layer(current)
        stored = record(stored, output, index, live)
        received = shifted(output, "segment", 1)
        return (received, stored)

    start_state = jnp.zeros((micro_rows, width), jnp.float32)
    unused, results = lax.fori_loop(0, steps, advance, (start_state, results))
    last = segment == segments - 1
    term = jnp.where(last, results, jnp.zeros(results.shape, jnp.float32))
    return lax.psum_scatter(term, "segment", scatter_dimension=0, tiled=True)


def solution(mesh):
    placed = (
        P(None, "col"),
        P("segment", "col", None, None),
        P("segment", "col"),
        P("segment", "col"),
        P("segment", "col"),
        P("segment", "col"),
    )
    return jax.shard_map(
        local, mesh=mesh, in_specs=placed, out_specs=P("segment", "col"), check_vma=False
    )
```

profile of v0, /device:TPU:239, one launch (start us, length us, event | category | flops | bytes accessed | tf_op | source)
XLA Modules:
  0.0 1689.5 jit_solution(17263489742637516951)
XLA Ops:
  21.3 17.1 %collective-permute-done.3 = f32[128,4096]{1,0:T(8,128)} collective-permute-done((f32[128,4096]{1,0:T(8,128)}, f32[128,4096]{1,0:T(8,128)}, u32[]{:S(2)}, u32[]{:S(2)}) %collective-permute-start.3) | collective-permute-done | bytes 2097184 | tf_op jit(solution)/shard_map/ppermute | solution.py:18
  50.3 1410.4 %while.17 = (s32[]{:T(128)}, f32[8,8192]{1,0:T(8,128)S(1)}, f32[128,8192]{1,0:T(8,128)}, s32[96]{0:T(128)S(1)}, pred[]{:T(512)}, /*index=5*/s32[]{:T(128)}, f32[...) while((s32[]{:T(128)}, f32[8,8192]{1,0:T(8,128)S(1)}, ...), condition=%wide.region_1.2_spmd.clone, body=%wide.region_0.1_spmd.clone.sunk | while | flops 227200880 | bytes 13802417 | solution.py:86
  212.0 8.4 collective-permute-done.2
  242.1 8.4 collective-permute-done.2
  272.2 8.4 collective-permute-done.2
  302.3 8.4 collective-permute-done.2
  422.6 8.4 collective-permute-done.2
  512.9 8.4 collective-permute-done.2
  543.0 8.4 collective-permute-done.2
  573.0 8.4 collective-permute-done.2
  723.5 8.4 collective-permute-done.2
  873.9 8.4 collective-permute-done.2
  1054.4 8.5 collective-permute-done.2
  1084.5 8.4 collective-permute-done.2
  1144.6 8.4 collective-permute-done.2
  1204.7 8.4 collective-permute-done.2
  1234.8 8.5 collective-permute-done.2
  1295.0 9.3 collective-permute-done.2
  1325.9 9.6 collective-permute-done.2
  1357.2 9.5 collective-permute-done.2
  1388.4 9.6 collective-permute-done.2
  1419.7 9.7 collective-permute-done.2
  1451.0 9.6 collective-permute-done.2
  1467.1 213.9 %all-reduce.3.cloned.1.call-done = f32[128,8192]{1,0:T(8,128)} async-done(((f32[128,8192]{1,0:T(8,128)}), f32[128,8192]{1,0:T(8,128)}) %all-reduce.3.cloned.1.call-update) | async-done | bytes 4194320
  (711 shorter events, 1255.4 us)
Async XLA Ops:
  6.5 1674.5 %all-reduce.3.cloned.1.call-start = ((), (), s32[]{:S(2)}) async-start(), calls=%async_computation | async-start | bytes 8388608
  11.3 27.0 %collective-permute-start.3 = (f32[128,4096]{1,0:T(8,128)}, f32[128,4096]{1,0:T(8,128)}, u32[]{:S(2)}, u32[]{:S(2)}) collective-permute-start(f32[128,4096]{1,0:T(8,128)} %get-tuple-element.260), channel_id=1, source_target_pairs={{0,1},{1,2},{2,3},{3,4},{4,5},{5,6},{6,7},{8,9},{9,10},{10,11},{11... | collective-permute-start | bytes 6291464 | tf_op jit(solution)/shard_map/ppermute | solution.py:18
  15.1 27.7 %collective-permute-start.4 = (f32[128,4096]{1,0:T(8,128)}, f32[128,4096]{1,0:T(8,128)}, u32[]{:S(2)}, u32[]{:S(2)}) collective-permute-start(f32[128,4096]{1,0:T(8,128)} %get-tuple-element.261), channel_id=1, source_target_pairs={{1,0},{2,1},{3,2},{4,3},{5,4},{6,5},{7,6},{9,8},{10,9},{11,10},{12... | collective-permute-start | bytes 6291464 | tf_op jit(solution)/shard_map/ppermute | solution.py:20
  210.7 9.7 collective-permute-start.2
  270.9 9.7 collective-permute-start.2
  301.0 9.7 collective-permute-start.2
  421.3 9.7 collective-permute-start.2
  511.6 9.7 collective-permute-start.2
  541.7 9.7 collective-permute-start.2
  571.7 9.7 collective-permute-start.2
  662.0 9.7 collective-permute-start.2
  722.2 9.7 collective-permute-start.2
  872.6 9.7 collective-permute-start.2
  1053.1 9.7 collective-permute-start.2
  1083.2 9.7 collective-permute-start.2
  1143.3 9.7 collective-permute-start.2
  1203.5 9.7 collective-permute-start.2
  1233.5 9.8 collective-permute-start.2
  1293.7 10.6 collective-permute-start.2
  1324.7 10.9 collective-permute-start.2
  1356.0 10.8 collective-permute-start.2
  1387.1 10.9 collective-permute-start.2
  1418.4 11.0 collective-permute-start.2
  1449.7 10.9 collective-permute-start.2
  (126 other events, 838.3 us)
Sparse Core Ops, SparseCore 0:
  1465.4 215.6 all-reduce.2
where the time goes:
time: 1710 us; the launch traced here: 1690 us
  waiting for transfers between devices  716 us (42%)
  starting transfers between devices  390 us (23%)
  matrix products  367 us (21%)
  other arithmetic  153 us (9%)
  local copies, waits for them, and re-layouts  43.4 us (3%)
    ppermute x47, waiting for transfers between devices, shifted(): return lax.ppermute(block, axis, route)  393 us
    dot_general x47, matrix products, layer(): jnp.einsum('rsk,skj->rsj', picked, weights, precision=lax.Precision.HIGHEST)  347 us
    ppermute x48, starting transfers between devices, extended_2(): lax.ppermute(head, axis, [((i + 1) % count, i) for i in range(ends)])  233 us
    unnamed x2, waiting for transfers between devices  214 us
    ppermute x48, starting transfers between devices, extended_2(): lax.ppermute(tail, axis, [(i, (i + 1) % count) for i in range(ends)])  96.9 us
    dynamic_update_slice x47, other arithmetic, record(): lax.dynamic_update_slice_in_dim(results, jnp.where(keep, output, former),...  87.5 us
    ppermute x48, waiting for transfers between devices, extended_2(): lax.ppermute(tail, axis, [(i, (i + 1) % count) for i in range(ends)])  74.3 us
    ppermute x47, starting transfers between devices, shifted(): return lax.ppermute(block, axis, route)  60.2 us
  transfers between devices with their start and end apart: 144, of which 144 were waited for; matrix products, arithmetic and copies ran while one was open for 0% of the time, Pallas kernels for 0%

commit v1 on v0

v1 whole, which is shorter than its diff:
```python
import functools

import jax
import jax.numpy as jnp
from jax import lax
from jax.experimental import pallas as pl
from jax.experimental.pallas import tpu as pltpu
from jax.sharding import PartitionSpec as P

REACH = 32
SEGS = 32
COLS = 8
OWN = 64
EXT = OWN + 2 * REACH
CAP = 96
TB = 128
ROWS = 128
R = 2
MICRO = ROWS // R
PARTS = 3
PAD = 8 if PARTS * R <= 8 else 16
FIN = ROWS // SEGS // R
MESH = pl.DeviceIdType.MESH
F32 = jnp.float32
BF16 = jnp.bfloat16


def kernel(
    order_ref, row_ref, same_ref, last_ref, acts_hbm, tiles_hbm, bias_ref, out_ref,
    acts, raw, weights, ext, held, picked, sums, fin,
    own_sem, halo_sem, fin_sem, send_sem, local_sem,
):
    seg = lax.axis_index("segment")
    col = lax.axis_index("col")
    is_first = seg == 0
    is_last = seg == SEGS - 1
    far = lax.rem(col, 2)
    near = 1 - far
    far_col = col - 1 + 2 * far
    near_col = col - 1 + 2 * near
    has_far = (far_col >= 0) & (far_col < COLS)

    tiles_copy = pltpu.make_async_copy(tiles_hbm, raw, local_sem.at[0])
    tiles_copy.start()
    acts_copy = pltpu.make_async_copy(acts_hbm, acts, local_sem.at[1])

    @pl.when(is_first)
    def _():
        acts_copy.start()

    barrier = pltpu.get_barrier_semaphore()

    def greet(s, c):
        pl.semaphore_signal(barrier, inc=1, device_id=(s, c), device_id_type=MESH)

    greet(seg, near_col)
    pl.when(has_far)(lambda: greet(seg, far_col))
    pl.when(seg > 0)(lambda: greet(seg - 1, col))
    pl.when(seg < SEGS - 1)(lambda: greet(SEGS - 1, col))

    tiles_copy.wait()
    for j in range(CAP):
        weights[j] = raw[order_ref[j]]
    sums[CAP] = jnp.zeros((PAD, TB), F32)

    pl.when(is_first)(lambda: acts_copy.wait())

    peers = 1 + has_far.astype(jnp.int32) + jnp.where(is_last, SEGS - 1, 1)
    pl.semaphore_wait(barrier, peers)

    def own_part(m, half):
        return ext.at[m, pl.ds(REACH + REACH * half, REACH)]

    def forward(m, half, target, sem):
        pltpu.make_async_remote_copy(
            src_ref=own_part(m, half),
            dst_ref=ext.at[m, pl.ds((EXT - REACH) * (1 - half), REACH)],
            send_sem=send_sem.at[sem],
            recv_sem=halo_sem.at[m, 1 - half],
            device_id=(seg, target),
            device_id_type=MESH,
        ).start()

    def await_own(m, half):
        part = own_part(m, half)
        pltpu.make_async_copy(part, part, own_sem.at[m, half]).wait()

    def receive(m):
        @pl.when(is_first)
        def _():
            for place in range(8 // R):
                @pl.when(lax.rem(m, 8 // R) == place)
                def _():
                    for b in range(OWN):
                        ext[m, REACH + b] = acts[
                            m // (8 // R), place * R:(place + 1) * R, b * TB:(b + 1) * TB
                        ]

        @pl.when(jnp.logical_not(is_first))
        def _():
            await_own(m, far)

        pl.when(has_far)(lambda: forward(m, far, far_col, 1))

        @pl.when(jnp.logical_not(is_first))
        def _():
            await_own(m, near)

        forward(m, near, near_col, 2)

    def await_halo(m):
        def one(side):
            part = ext.at[m, pl.ds((EXT - REACH) * side, REACH)]
            pltpu.make_async_copy(part, part, halo_sem.at[m, side]).wait()

        one(near)
        pl.when(has_far)(lambda: one(far))

    sub = lax.broadcasted_iota(jnp.int32, (PAD, TB), 0)

    def split(x):
        x = jnp.concatenate([x] * (PAD // R), axis=0)
        high = x.astype(BF16).astype(F32)
        rest = x - high
        middle = rest.astype(BF16).astype(F32)
        low = rest - middle
        parts = jnp.where(sub < R, high, jnp.where(sub < 2 * R, middle, jnp.where(sub < 3 * R, low, 0.0)))
        return parts.astype(BF16)

    def compute(m):
        picked[...] = ext[m]
        run = jnp.zeros((PAD, TB), F32)
        for j in range(0, CAP, 2):
            a = split(picked[row_ref[j]])
            b = split(picked[row_ref[j + 1]])
            zero = jnp.zeros_like(a)
            left = jnp.concatenate(
                [jnp.concatenate([a, zero], 1), jnp.concatenate([zero, b], 1)], 0
            )
            right = weights[j:j + 2].reshape(2 * TB, TB)
            prod = jnp.dot(left, right, preferred_element_type=F32)
            run = jnp.where(same_ref[j] != 0, run, 0.0) + prod[:PAD]
            sums[j] = run
            run = jnp.where(same_ref[j + 1] != 0, run, 0.0) + prod[PAD:]
            sums[j + 1] = run
        for c in range(OWN):
            v = sums[last_ref[c]]
            total = v[0:R] + v[R:2 * R]
            if PARTS == 3:
                total = total + v[2 * R:3 * R]
            held[m, c] = jnp.clip(total + bias_ref[0:1, c * TB:(c + 1) * TB], 0.0, 32.0)

    def send(m):
        @pl.when(jnp.logical_not(is_last))
        def _():
            for half in (far, near):
                pltpu.make_async_remote_copy(
                    src_ref=held.at[m, pl.ds(REACH * half, REACH)],
                    dst_ref=own_part(m, half),
                    send_sem=send_sem.at[0],
                    recv_sem=own_sem.at[m, half],
                    device_id=(seg + 1, col),
                    device_id_type=MESH,
                ).start()

        target = m // FIN
        place = lax.rem(m, FIN)

        @pl.when(is_last & (target < SEGS - 1))
        def _():
            pltpu.make_async_remote_copy(
                src_ref=held.at[m],
                dst_ref=fin.at[place],
                send_sem=send_sem.at[0],
                recv_sem=fin_sem.at[place],
                device_id=(target, col),
                device_id_type=MESH,
            ).start()

        @pl.when(is_last & (target == SEGS - 1))
        def _():
            pltpu.make_async_copy(held.at[m], fin.at[place], fin_sem.at[place]).start()

    receive(0)

    def step(m, carry):
        await_halo(m)
        pl.when(m + 1 < MICRO)(lambda: receive(m + 1))
        compute(m)
        send(m)
        return carry

    lax.fori_loop(0, MICRO, step, 0)

    for place in range(FIN):
        pltpu.make_async_copy(fin.at[place], fin.at[place], fin_sem.at[place]).wait()
        for c in range(OWN):
            out_ref[place * R:(place + 1) * R, c * TB:(c + 1) * TB] = fin[place, c]

    def drain(part, sem):
        pltpu.make_async_copy(part, part, send_sem.at[sem]).wait()

    @pl.when(is_last)
    def _():
        drain(held.at[pl.ds(0, MICRO - FIN)], 0)

    @pl.when(jnp.logical_not(is_last))
    def _():
        drain(held, 0)

    pl.when(has_far)(lambda: drain(ext.at[:, pl.ds(0, REACH)], 1))
    drain(ext.at[:, pl.ds(0, REACH)], 2)


def prepare(tile_row, tile_col, tile_count):
    column = lax.axis_index("col")
    slots = jnp.arange(CAP, dtype=jnp.int32)
    valid = slots < tile_count[0, 0]
    row = jnp.where(valid, tile_row[0] - column * OWN + REACH, REACH)
    target = jnp.where(valid, tile_col[0], OWN)
    key = target * CAP + slots
    rank = jnp.sum((key[None, :] < key[:, None]).astype(jnp.int32), axis=1)
    place = rank[None, :] == slots[:, None]

    def ordered(values):
        return jnp.sum(jnp.where(place, values[None, :], 0), axis=1)

    order, row, target_sorted = ordered(slots), ordered(row), ordered(target)
    former = jnp.concatenate([jnp.full((1,), -1, jnp.int32), target_sorted[:-1]])
    same = (target_sorted == former).astype(jnp.int32)
    blocks = jnp.arange(OWN, dtype=jnp.int32)
    count = jnp.sum((target[None, :] == blocks[:, None]).astype(jnp.int32), axis=1)
    upto = jnp.sum((target[None, :] <= blocks[:, None]).astype(jnp.int32), axis=1)
    last = jnp.where(count > 0, upto - 1, CAP)
    return order, row, same, last


def local(acts, tiles, tile_row, tile_col, tile_count, bias):
    tables = prepare(tile_row, tile_col, tile_count)
    smem = pl.BlockSpec(memory_space=pltpu.SMEM)
    vmem = pl.BlockSpec(memory_space=pltpu.VMEM)
    hbm = pl.BlockSpec(memory_space=pl.ANY)
    dma = pltpu.SemaphoreType.DMA
    return pl.pallas_call(
        kernel,
        out_shape=jax.ShapeDtypeStruct((ROWS // SEGS, OWN * TB), F32),
        in_specs=[smem, smem, smem, smem, hbm, hbm, vmem],
        out_specs=vmem,
        scratch_shapes=[
            pltpu.VMEM((ROWS // 8, 8, OWN * TB), F32),
            pltpu.VMEM((CAP, TB, TB), BF16),
            pltpu.VMEM((CAP, TB, TB), BF16),
            pltpu.VMEM((MICRO, EXT, R, TB), F32),
            pltpu.VMEM((MICRO, OWN, R, TB), F32),
            pltpu.VMEM((EXT, R, TB), F32),
            pltpu.VMEM((CAP + 1, PAD, TB), F32),
            pltpu.VMEM((FIN, OWN, R, TB), F32),
            dma((MICRO, 2)),
            dma((MICRO, 2)),
            dma((FIN,)),
            dma((3,)),
            dma((2,)),
        ],
        compiler_params=pltpu.CompilerParams(
            collective_id=0, has_side_effects=True, vmem_limit_bytes=48 << 20
        ),
        cost_estimate=pl.CostEstimate(
            flops=2 * ROWS * CAP * TB * TB, bytes_accessed=8 << 20, transcendentals=0
        ),
    )(*tables, acts.reshape(ROWS // 8, 8, OWN * TB), tiles[0], bias)


def solution(mesh):
    placed = (
        P(None, "col"),
        P("segment", "col", None, None),
        P("segment", "col"),
        P("segment", "col"),
        P("segment", "col"),
        P("segment", "col"),
    )
    return jax.shard_map(
        local, mesh=mesh, in_specs=placed, out_specs=P("segment", "col"), check_vma=False
    )
```

time: 1710 us -> 393 us (0.23); the launches traced: 1690 us -> 391 us
  waiting for transfers between devices: 716 us -> 0 us
  starting transfers between devices: 390 us -> 0 us
  Pallas kernels: 0 us -> 385 us
  matrix products: 367 us -> 0 us
  other arithmetic: 153 us -> 1.86 us
  local copies, waits for them, and re-layouts: 43.4 us -> 3.3 us
    ppermute x143 -> x0, waiting for transfers between devices: 502 us -> none  [the longest x47 393 us: shifted(): return lax.ppermute(block, axis, route)]
    ppermute x143 -> x0, starting transfers between devices: 390 us -> none  [the longest x48 233 us: extended_2(): lax.ppermute(head, axis, [((i + 1) % count, i) for i in range(ends)])]
    pallas_call x0 -> x1, Pallas kernels: none -> 385 us  [local(): pl.pallas_call(kernel, out_shape=jax.ShapeDtypeStruct((ROWS // SEGS, OWN...]
    dot_general x94 -> x0, matrix products: 367 us -> none  [the longest x47 347 us: layer(): jnp.einsum('rsk,skj->rsj', picked, weights, precision=lax.Precision.HIGHEST)]
    unnamed x2 -> x0, waiting for transfers between devices: 214 us -> none
    dynamic_update_slice x47 -> x0, other arithmetic: 87.5 us -> none  [record(): lax.dynamic_update_slice_in_dim(results, jnp.where(keep, output, former),...]
    reshape x47 -> x0, other arithmetic: 51.6 us -> none  [layer(): blocks = extended.reshape(micro_rows, own_blocks + 2 * REACH, tile_size)]
    gather x47 -> x0, local copies, waits for them, and re-layouts: 32.5 us -> none  [layer(): picked = jnp.take(blocks, local_rows, axis=1)]
  transfers between devices with their start and end apart: 144 -> 0, of which waited for: 144 -> 0; matrix products, arithmetic and copies ran while one was open for 0% -> 0% of each run, Pallas kernels for 0% -> 0%
where the time goes in v1:
time: 393 us; the launch traced here: 391 us
  Pallas kernels  385 us (98%)
    pallas_call x1, Pallas kernels, local(): pl.pallas_call(kernel, out_shape=jax.ShapeDtypeStruct((ROWS // SEGS, OWN...  385 us

profile of v1, /device:TPU:239, one launch (start us, length us, event | category | flops | bytes accessed | tf_op | source)
XLA Modules:
  0.0 391.2 jit_solution(6795272684314058627)
XLA Ops:
  0.7 0.7 fusion.2
  1.3 0.7 add_bitcast_fusion
  2.0 0.2 convert_reduce_fusion
  2.2 0.2 select_reduce_fusion
  2.3 0.1 compare_convert_fusion.same_ref
  2.4 0.1 convert_reduce_fusion.1
  2.5 0.0 copy-start
  2.5 1.9 copy-done
  4.4 0.0 copy-start.1
  4.4 0.8 copy-done.1
  5.2 385.3 %shard_map.64 = f32[4,8192]{1,0:T(4,128)S(1)} custom-call(s32[96]{0:T(128)S(1)} %get-tuple-element.9.order_ref, s32[96]{0:T(128)S(1)} %get-tuple-element.8.row_ref, s32[96]{0:T(128)S(1)} %compare_convert_fusion.same_ref, s32[64]{0:T(128)S(1)} %compare_select_fusion.last_ref, f32[16,8,8192]{2,1,0:T(8,128)} %bitcast.15, bf16[96,128,128]{2,1,0:T(8,128)(2,1)S(1)} %bitcast.14, ...), custom_call_target="tpu_custom_call" | custom-call | flops 402653184 | bytes 8388608 | tf_op jit(solution)/shard_map/pallas_call | solution.py:244
  390.5 0.7 copy.9
  (1 shorter events, 0.0 us)
Async XLA Ops:
  2.5 1.9 copy-start
  4.4 0.8 copy-start.1

commit v2 on v1

--- a/solution.py
+++ b/solution.py
@@ -15,11 +15,13 @@
 CAP = 96
 TB = 128
 ROWS = 128
-R = 2
+R = 1
 MICRO = ROWS // R
 PARTS = 3
 PAD = 8 if PARTS * R <= 8 else 16
 FIN = ROWS // SEGS // R
+RELAY = True
+AHEAD = 8 // R
 MESH = pl.DeviceIdType.MESH
 F32 = jnp.float32
 BF16 = jnp.bfloat16
@@ -53,9 +55,21 @@
     def greet(s, c):
         pl.semaphore_signal(barrier, inc=1, device_id=(s, c), device_id_type=MESH)
 
-    greet(seg, near_col)
-    pl.when(has_far)(lambda: greet(seg, far_col))
-    pl.when(seg > 0)(lambda: greet(seg - 1, col))
+    @pl.when(seg > 0)
+    def _():
+        greet(seg - 1, col)
+        if not RELAY:
+            greet(seg - 1, near_col)
+        pl.when(has_far)(lambda: greet(seg - 1, far_col))
+
+    @pl.when(is_first)
+    def _():
+        pl.when(has_far)(lambda: greet(seg, far_col))
+        if not RELAY:
+            greet(seg, near_col)
+
+    if RELAY:
+        greet(seg, near_col)
     pl.when(seg < SEGS - 1)(lambda: greet(SEGS - 1, col))
 
     tiles_copy.wait()
@@ -65,52 +79,61 @@
 
     pl.when(is_first)(lambda: acts_copy.wait())
 
-    peers = 1 + has_far.astype(jnp.int32) + jnp.where(is_last, SEGS - 1, 1)
+    reach = has_far.astype(jnp.int32)
+    if RELAY:
+        peers = 1 + jnp.where(is_last, SEGS - 1, 1 + reach + jnp.where(is_first, reach, 0))
+    else:
+        peers = jnp.where(is_last, SEGS - 1, 2 + reach + jnp.where(is_first, 1 + reach, 0))
     pl.semaphore_wait(barrier, peers)
 
     def own_part(m, half):
         return ext.at[m, pl.ds(REACH + REACH * half, REACH)]
 
-    def forward(m, half, target, sem):
+    def rim_part(m, side):
+        return ext.at[m, pl.ds((EXT - REACH) * side, REACH)]
+
+    def push(source, target, landing, sent, landed):
         pltpu.make_async_remote_copy(
-            src_ref=own_part(m, half),
-            dst_ref=ext.at[m, pl.ds((EXT - REACH) * (1 - half), REACH)],
-            send_sem=send_sem.at[sem],
-            recv_sem=halo_sem.at[m, 1 - half],
-            device_id=(seg, target),
+            src_ref=source,
+            dst_ref=landing,
+            send_sem=send_sem.at[sent],
+            recv_sem=landed,
+            device_id=target,
             device_id_type=MESH,
         ).start()
+
+    def push_rim(source, m, half, target, sent):
+        push(source, target, rim_part(m, 1 - half), sent, halo_sem.at[m, 1 - half])
 
     def await_own(m, half):
         part = own_part(m, half)
         pltpu.make_async_copy(part, part, own_sem.at[m, half]).wait()
 
-    def receive(m):
-        @pl.when(is_first)
-        def _():
-            for place in range(8 // R):
-                @pl.when(lax.rem(m, 8 // R) == place)
-                def _():
-                    for b in range(OWN):
-                        ext[m, REACH + b] = acts[
-                            m // (8 // R), place * R:(place + 1) * R, b * TB:(b + 1) * TB
-                        ]
-
+    def load_first(m):
+        for place in range(8 // R):
+            @pl.when(lax.rem(m, 8 // R) == place)
+            def _():
+                for b in range(OWN):
+                    ext[m, REACH + b] = acts[
+                        m // (8 // R), place * R:(place + 1) * R, b * TB:(b + 1) * TB
+                    ]
+
+        pl.when(has_far)(lambda: push_rim(own_part(m, far), m, far, (seg, far_col), 3))
+        push_rim(own_part(m, near), m, near, (seg, near_col), 4)
+
+    def relay(m):
+        await_own(m, near)
+        push_rim(own_part(m, near), m, near, (seg, near_col), 2)
+
+    def await_input(m):
         @pl.when(jnp.logical_not(is_first))
         def _():
+            if not RELAY:
+                await_own(m, near)
             await_own(m, far)
 
-        pl.when(has_far)(lambda: forward(m, far, far_col, 1))
-
-        @pl.when(jnp.logical_not(is_first))
-        def _():
-            await_own(m, near)
-
-        forward(m, near, near_col, 2)
-
-    def await_halo(m):
         def one(side):
-            part = ext.at[m, pl.ds((EXT - REACH) * side, REACH)]
+            part = rim_part(m, side)
             pltpu.make_async_copy(part, part, halo_sem.at[m, side]).wait()
 
         one(near)
@@ -153,15 +176,19 @@
     def send(m):
         @pl.when(jnp.logical_not(is_last))
         def _():
-            for half in (far, near):
-                pltpu.make_async_remote_copy(
-                    src_ref=held.at[m, pl.ds(REACH * half, REACH)],
-                    dst_ref=own_part(m, half),
-                    send_sem=send_sem.at[0],
-                    recv_sem=own_sem.at[m, half],
-                    device_id=(seg + 1, col),
-                    device_id_type=MESH,
-                ).start()
+            def half_of(half):
+                return held.at[m, pl.ds(REACH * half, REACH)]
+
+            def push_own(half):
+                push(half_of(half), (seg + 1, col), own_part(m, half), 0, own_sem.at[m, half])
+
+            if RELAY:
+                push_own(near)
+            pl.when(has_far)(lambda: push_rim(half_of(far), m, far, (seg + 1, far_col), 1))
+            push_own(far)
+            if not RELAY:
+                push_own(near)
+                push_rim(half_of(near), m, near, (seg + 1, near_col), 2)
 
         target = m // FIN
         place = lax.rem(m, FIN)
@@ -181,11 +208,19 @@
         def _():
             pltpu.make_async_copy(held.at[m], fin.at[place], fin_sem.at[place]).start()
 
-    receive(0)
+    @pl.when(is_first)
+    def _():
+        for m in range(AHEAD):
+            load_first(m)
+
+    if RELAY:
+        pl.when(jnp.logical_not(is_first))(lambda: relay(0))
 
     def step(m, carry):
-        await_halo(m)
-        pl.when(m + 1 < MICRO)(lambda: receive(m + 1))
+        pl.when(is_first & (m + AHEAD < MICRO))(lambda: load_first(m + AHEAD))
+        if RELAY:
+            pl.when(jnp.logical_not(is_first) & (m + 1 < MICRO))(lambda: relay(m + 1))
+        await_input(m)
         compute(m)
         send(m)
         return carry
@@ -200,6 +235,8 @@
     def drain(part, sem):
         pltpu.make_async_copy(part, part, send_sem.at[sem]).wait()
 
+    half_shape = held.at[:, pl.ds(0, REACH)]
+
     @pl.when(is_last)
     def _():
         drain(held.at[pl.ds(0, MICRO - FIN)], 0)
@@ -207,9 +244,17 @@
     @pl.when(jnp.logical_not(is_last))
     def _():
         drain(held, 0)
-
-    pl.when(has_far)(lambda: drain(ext.at[:, pl.ds(0, REACH)], 1))
-    drain(ext.at[:, pl.ds(0, REACH)], 2)
+        pl.when(has_far)(lambda: drain(half_shape, 1))
+        if not RELAY:
+            drain(half_shape, 2)
+
+    if RELAY:
+        pl.when(jnp.logical_not(is_first))(lambda: drain(half_shape, 2))
+
+    @pl.when(is_first)
+    def _():
+        pl.when(has_far)(lambda: drain(half_shape, 3))
+        drain(half_shape, 4)
 
 
 def prepare(tile_row, tile_col, tile_count):
@@ -258,7 +303,7 @@
             dma((MICRO, 2)),
             dma((MICRO, 2)),
             dma((FIN,)),
-            dma((3,)),
+            dma((5,)),
             dma((2,)),
         ],
         compiler_params=pltpu.CompilerParams(

time: 393 us -> 293 us (0.75)
  Pallas kernels: 385 us -> 287 us
    pallas_call x1, Pallas kernels: 385 us -> 287 us  [local(): pl.pallas_call(kernel, out_shape=jax.ShapeDtypeStruct((ROWS // SEGS, OWN...]
where the time goes in v2:
time: 293 us
  Pallas kernels  287 us (98%)
  local copies, waits for them, and re-layouts  3.3 us (1%)
    pallas_call x1, Pallas kernels, local(): pl.pallas_call(kernel, out_shape=jax.ShapeDtypeStruct((ROWS // SEGS, OWN...  287 us

profile of v2, /device:TPU:239, one launch (start us, length us, event | category | flops | bytes accessed | tf_op | source)
XLA Modules:
  0.0 292.7 jit_solution(5623908628881268983)
XLA Ops:
  0.7 0.7 fusion.2
  1.3 0.7 add_bitcast_fusion
  2.0 0.2 convert_reduce_fusion
  2.2 0.2 select_reduce_fusion
  2.3 0.1 compare_convert_fusion.same_ref
  2.4 0.1 convert_reduce_fusion.1
  2.5 0.0 copy-start
  2.5 1.9 copy-done
  4.4 0.0 copy-start.1
  4.4 0.8 copy-done.1
  5.2 286.9 %shard_map.64 = f32[4,8192]{1,0:T(4,128)S(1)} custom-call(s32[96]{0:T(128)S(1)} %get-tuple-element.9.order_ref, s32[96]{0:T(128)S(1)} %get-tuple-element.8.row_ref, s32[96]{0:T(128)S(1)} %compare_convert_fusion.same_ref, s32[64]{0:T(128)S(1)} %compare_select_fusion.last_ref, f32[16,8,8192]{2,1,0:T(8,128)} %bitcast.15, bf16[96,128,128]{2,1,0:T(8,128)(2,1)S(1)} %bitcast.14, ...), custom_call_target="tpu_custom_call" | custom-call | flops 402653184 | bytes 8388608 | tf_op jit(solution)/shard_map/pallas_call | solution.py:289
  292.1 0.7 copy.9
  (1 shorter events, 0.0 us)
Async XLA Ops:
  2.5 1.9 copy-start
  4.4 0.8 copy-start.1

commit v3 on v2

--- a/solution.py
+++ b/solution.py
@@ -17,8 +17,7 @@
 ROWS = 128
 R = 1
 MICRO = ROWS // R
-PARTS = 3
-PAD = 8 if PARTS * R <= 8 else 16
+PAD = 8
 FIN = ROWS // SEGS // R
 RELAY = True
 AHEAD = 8 // R
@@ -28,8 +27,8 @@
 
 
 def kernel(
-    order_ref, row_ref, same_ref, last_ref, acts_hbm, tiles_hbm, bias_ref, out_ref,
-    acts, raw, weights, ext, held, picked, sums, fin,
+    order_ref, row_ref, same_ref, last_ref, acts_hbm, tiles_hbm, bias_hbm, out_ref,
+    acts, raw, weights, bias, ext, held, picked, sums, ends, fin,
     own_sem, halo_sem, fin_sem, send_sem, local_sem,
 ):
     seg = lax.axis_index("segment")
@@ -44,6 +43,8 @@
 
     tiles_copy = pltpu.make_async_copy(tiles_hbm, raw, local_sem.at[0])
     tiles_copy.start()
+    bias_copy = pltpu.make_async_copy(bias_hbm, bias, local_sem.at[2])
+    bias_copy.start()
     acts_copy = pltpu.make_async_copy(acts_hbm, acts, local_sem.at[1])
 
     @pl.when(is_first)
@@ -76,6 +77,7 @@
     for j in range(CAP):
         weights[j] = raw[order_ref[j]]
     sums[CAP] = jnp.zeros((PAD, TB), F32)
+    bias_copy.wait()
 
     pl.when(is_first)(lambda: acts_copy.wait())
 
@@ -87,10 +89,10 @@
     pl.semaphore_wait(barrier, peers)
 
     def own_part(m, half):
-        return ext.at[m, pl.ds(REACH + REACH * half, REACH)]
+        return ext.at[m, pl.ds(pl.multiple_of(REACH + REACH * half, REACH), REACH)]
 
     def rim_part(m, side):
-        return ext.at[m, pl.ds((EXT - REACH) * side, REACH)]
+        return ext.at[m, pl.ds(pl.multiple_of((EXT - REACH) * side, REACH), REACH)]
 
     def push(source, target, landing, sent, landed):
         pltpu.make_async_remote_copy(
@@ -114,7 +116,7 @@
             @pl.when(lax.rem(m, 8 // R) == place)
             def _():
                 for b in range(OWN):
-                    ext[m, REACH + b] = acts[
+                    ext[m, REACH + b:REACH + b + 1] = acts[
                         m // (8 // R), place * R:(place + 1) * R, b * TB:(b + 1) * TB
                     ]
 
@@ -140,44 +142,40 @@
         pl.when(has_far)(lambda: one(far))
 
     sub = lax.broadcasted_iota(jnp.int32, (PAD, TB), 0)
-
-    def split(x):
-        x = jnp.concatenate([x] * (PAD // R), axis=0)
+    zero = jnp.zeros((PAD, TB), F32)
+
+    def split(j):
+        x = jnp.broadcast_to(picked[row_ref[j]].reshape(1, TB), (PAD, TB))
         high = x.astype(BF16).astype(F32)
-        rest = x - high
-        middle = rest.astype(BF16).astype(F32)
-        low = rest - middle
-        parts = jnp.where(sub < R, high, jnp.where(sub < 2 * R, middle, jnp.where(sub < 3 * R, low, 0.0)))
-        return parts.astype(BF16)
+        return jnp.where(sub < 1, high, jnp.where(sub < 2, x - high, 0.0))
 
     def compute(m):
         picked[...] = ext[m]
-        run = jnp.zeros((PAD, TB), F32)
+        run = zero
         for j in range(0, CAP, 2):
-            a = split(picked[row_ref[j]])
-            b = split(picked[row_ref[j + 1]])
-            zero = jnp.zeros_like(a)
-            left = jnp.concatenate(
-                [jnp.concatenate([a, zero], 1), jnp.concatenate([zero, b], 1)], 0
+            upper = jnp.concatenate([split(j), zero], 0).astype(BF16)
+            lower = jnp.concatenate([zero, split(j + 1)], 0).astype(BF16)
+            prod = jnp.dot(
+                jnp.concatenate([upper, lower], 1),
+                weights[j:j + 2].reshape(2 * TB, TB),
+                preferred_element_type=F32,
             )
-            right = weights[j:j + 2].reshape(2 * TB, TB)
-            prod = jnp.dot(left, right, preferred_element_type=F32)
             run = jnp.where(same_ref[j] != 0, run, 0.0) + prod[:PAD]
             sums[j] = run
             run = jnp.where(same_ref[j + 1] != 0, run, 0.0) + prod[PAD:]
             sums[j + 1] = run
         for c in range(OWN):
-            v = sums[last_ref[c]]
-            total = v[0:R] + v[R:2 * R]
-            if PARTS == 3:
-                total = total + v[2 * R:3 * R]
-            held[m, c] = jnp.clip(total + bias_ref[0:1, c * TB:(c + 1) * TB], 0.0, 32.0)
+            ends[c * PAD:(c + 1) * PAD] = sums[last_ref[c]]
+        for c in range(0, OWN, 8):
+            high = ends[pl.ds(c * PAD, 8, stride=PAD), :]
+            low = ends[pl.ds(c * PAD + 1, 8, stride=PAD), :]
+            held[m, c:c + 8] = jnp.clip(high + low + bias[c:c + 8], 0.0, 32.0)
 
     def send(m):
         @pl.when(jnp.logical_not(is_last))
         def _():
             def half_of(half):
-                return held.at[m, pl.ds(REACH * half, REACH)]
+                return held.at[m, pl.ds(pl.multiple_of(REACH * half, REACH), REACH)]
 
             def push_own(half):
                 push(half_of(half), (seg + 1, col), own_part(m, half), 0, own_sem.at[m, half])
@@ -230,7 +228,7 @@
     for place in range(FIN):
         pltpu.make_async_copy(fin.at[place], fin.at[place], fin_sem.at[place]).wait()
         for c in range(OWN):
-            out_ref[place * R:(place + 1) * R, c * TB:(c + 1) * TB] = fin[place, c]
+            out_ref[place * R:(place + 1) * R, c * TB:(c + 1) * TB] = fin[place, c:c + 1]
 
     def drain(part, sem):
         pltpu.make_async_copy(part, part, send_sem.at[sem]).wait()
@@ -289,30 +287,32 @@
     return pl.pallas_call(
         kernel,
         out_shape=jax.ShapeDtypeStruct((ROWS // SEGS, OWN * TB), F32),
-        in_specs=[smem, smem, smem, smem, hbm, hbm, vmem],
+        in_specs=[smem, smem, smem, smem, hbm, hbm, hbm],
         out_specs=vmem,
         scratch_shapes=[
             pltpu.VMEM((ROWS // 8, 8, OWN * TB), F32),
             pltpu.VMEM((CAP, TB, TB), BF16),
             pltpu.VMEM((CAP, TB, TB), BF16),
-            pltpu.VMEM((MICRO, EXT, R, TB), F32),
-            pltpu.VMEM((MICRO, OWN, R, TB), F32),
-            pltpu.VMEM((EXT, R, TB), F32),
+            pltpu.VMEM((OWN, TB), F32),
+            pltpu.VMEM((MICRO, EXT, TB), F32),
+            pltpu.VMEM((MICRO, OWN, TB), F32),
+            pltpu.VMEM((EXT, TB), F32),
             pltpu.VMEM((CAP + 1, PAD, TB), F32),
-            pltpu.VMEM((FIN, OWN, R, TB), F32),
+            pltpu.VMEM((OWN * PAD, TB), F32),
+            pltpu.VMEM((FIN, OWN, TB), F32),
             dma((MICRO, 2)),
             dma((MICRO, 2)),
             dma((FIN,)),
             dma((5,)),
-            dma((2,)),
+            dma((3,)),
         ],
         compiler_params=pltpu.CompilerParams(
-            collective_id=0, has_side_effects=True, vmem_limit_bytes=48 << 20
+            collective_id=0, has_side_effects=True, vmem_limit_bytes=60 << 20
         ),
         cost_estimate=pl.CostEstimate(
             flops=2 * ROWS * CAP * TB * TB, bytes_accessed=8 << 20, transcendentals=0
         ),
-    )(*tables, acts.reshape(ROWS // 8, 8, OWN * TB), tiles[0], bias)
+    )(*tables, acts.reshape(ROWS // 8, 8, OWN * TB), tiles[0], bias.reshape(OWN, TB))
 
 
 def solution(mesh):

time: 293 us -> 291 us (level)
  no operation moved by 1% of the time
where the time goes in v3:
time: 291 us
  Pallas kernels  285 us (98%)
  other arithmetic  3.49 us (1%)
    pallas_call x1, Pallas kernels, local(): pl.pallas_call(kernel, out_shape=jax.ShapeDtypeStruct((ROWS // SEGS, OWN...  285 us

profile of v3, /device:TPU:239, one launch (start us, length us, event | category | flops | bytes accessed | tf_op | source)
XLA Modules:
  0.0 290.8 jit_solution(1471011900920749851)
XLA Ops:
  0.7 0.7 fusion.2
  1.3 0.7 add_bitcast_fusion
  2.0 0.2 convert_reduce_fusion
  2.2 0.6 select_reduce_fusion
  2.8 0.7 compare_convert_fusion.same_ref
  3.5 0.1 convert_reduce_fusion.1
  3.6 0.6 compare_select_fusion.last_ref
  4.1 285.0 %shard_map.64 = f32[4,8192]{1,0:T(4,128)} custom-call(s32[96]{0:T(128)} %get-tuple-element.9.order_ref, s32[96]{0:T(128)} %get-tuple-element.8.row_ref, s32[96]{0:T(128)} %compare_convert_fusion.same_ref, s32[64]{0:T(128)} %compare_select_fusion.last_ref, f32[16,8,8192]{2,1,0:T(8,128)} %bitcast.15, bf16[96,128,128]{2,1,0:T(8,128)(2,1)} %bitcast.16, ...), custom_call_target="tpu_custom_call" | custom-call | flops 402653184 | bytes 8388608 | tf_op jit(solution)/shard_map/pallas_call | solution.py:287
  289.2 1.6 copy.9

commit v4 on v3

--- a/solution.py
+++ b/solution.py
@@ -20,7 +20,7 @@
 PAD = 8
 FIN = ROWS // SEGS // R
 RELAY = True
-AHEAD = 8 // R
+AHEAD = 4
 MESH = pl.DeviceIdType.MESH
 F32 = jnp.float32
 BF16 = jnp.bfloat16
@@ -72,12 +72,6 @@
     if RELAY:
         greet(seg, near_col)
     pl.when(seg < SEGS - 1)(lambda: greet(SEGS - 1, col))
-
-    tiles_copy.wait()
-    for j in range(CAP):
-        weights[j] = raw[order_ref[j]]
-    sums[CAP] = jnp.zeros((PAD, TB), F32)
-    bias_copy.wait()
 
     pl.when(is_first)(lambda: acts_copy.wait())
 
@@ -206,9 +200,17 @@
         def _():
             pltpu.make_async_copy(held.at[m], fin.at[place], fin_sem.at[place]).start()
 
+    pl.when(is_first)(lambda: load_first(0))
+
+    tiles_copy.wait()
+    for j in range(CAP):
+        weights[j] = raw[order_ref[j]]
+    sums[CAP] = jnp.zeros((PAD, TB), F32)
+    bias_copy.wait()
+
     @pl.when(is_first)
     def _():
-        for m in range(AHEAD):
+        for m in range(1, AHEAD):
             load_first(m)
 
     if RELAY:

time: 291 us -> 291 us (level)
  no operation moved by 1% of the time
where the time goes in v4:
time: 291 us
  Pallas kernels  285 us (98%)
  other arithmetic  3.49 us (1%)
    pallas_call x1, Pallas kernels, local(): pl.pallas_call(kernel, out_shape=jax.ShapeDtypeStruct((ROWS // SEGS, OWN...  285 us

profile of v4, /device:TPU:239, one launch (start us, length us, event | category | flops | bytes accessed | tf_op | source)
XLA Modules:
  0.0 290.8 jit_solution(12813127031545291037)
XLA Ops:
  0.7 0.7 fusion.2
  1.3 0.7 add_bitcast_fusion
  2.0 0.2 convert_reduce_fusion
  2.2 0.6 select_reduce_fusion
  2.8 0.7 compare_convert_fusion.same_ref
  3.5 0.1 convert_reduce_fusion.1
  3.6 0.6 compare_select_fusion.last_ref
  4.1 285.0 %shard_map.64 = f32[4,8192]{1,0:T(4,128)} custom-call(s32[96]{0:T(128)} %get-tuple-element.9.order_ref, s32[96]{0:T(128)} %get-tuple-element.8.row_ref, s32[96]{0:T(128)} %compare_convert_fusion.same_ref, s32[64]{0:T(128)} %compare_select_fusion.last_ref, f32[16,8,8192]{2,1,0:T(8,128)} %bitcast.15, bf16[96,128,128]{2,1,0:T(8,128)(2,1)} %bitcast.16, ...), custom_call_target="tpu_custom_call" | custom-call | flops 402653184 | bytes 8388608 | tf_op jit(solution)/shard_map/pallas_call | solution.py:289
  289.2 1.6 copy.9
